TPU v7x, 32 devices: a whole 2x2x4 slice. The times are simulated.
32 devices in a mesh: parts: 2 (over y), row: 4 (over x, core), col: 4 (over z).
Axes of the slice: x: 2, y: 2, z: 4, core: 2. Of those that a mesh axis runs over, the one named last changes fastest.
Arguments:
- tiles: bfloat16 [8, 4, 96, 128, 128], P(('parts', 'row'), 'col'), parts along dimension 0, may hold values from 0 to 6, as said below
- tile_rows: int32 [8, 4, 96], P(('parts', 'row'), 'col'), parts along dimension 0, may hold values from 0 to 63, as said below
- tile_cols: int32 [8, 4, 96], P(('parts', 'row'), 'col'), parts along dimension 0, may hold values from 0 to 63
- tile_counts: int32 [8, 4], P(('parts', 'row'), 'col'), parts along dimension 0, may hold values from 1 to 96, as said below
- seed_pages: int32 [16, 32], P('parts'), parts along dimension 0, may hold values from 0 to 32767, as said below
- seed_mass: float32 [16, 32], P('parts'), parts along dimension 0, may hold values from 4 to 32
- heat_time: float32 [16], P('parts'), parts along dimension 0, may hold values from 1 to 4
Outputs:
- heat: float32 [512, 8, 128], P(('parts', 'row', 'col')), parts along dimension 0
There are 2 independent parts, one for each index of `parts`. A program takes and returns all parts, laid end to end along the dimension named above; each array names one. Nothing has to cross between parts.
Inputs may be any that keep to these rules, and one draw needn't show every extreme that they name: `tile_counts`: at least one device holds exactly 96 used slots. The pairs (tile_rows, tile_cols) of one device's 96 slots are all distinct. `tiles`: entries are zero or positive. `seed_pages`: seed k of every set lies in piece number k mod 16 (pieces numbered r * 4 + c).
All inputs are finite; a program needn't handle non-finite values.
Results may differ from a plain program's by a relative error of at most 0.005.
Values may be sent and summed in bfloat16 or wider, within the bound.
A program may use at most 64 MiB of HBM per device.

v0:
```python
import jax
import jax.numpy as jnp
from jax import lax
from jax.sharding import PartitionSpec as P

PB = 16
K_TERMS = 3


def tile_image(column_z, tile_set, rows_index, cols_index, valid, row_blocks):
    picked = jnp.take(column_z, cols_index, axis=0)
    prod = jnp.einsum("tsb,tab->tsa", picked, tile_set, preferred_element_type=jnp.float32)
    prod = prod * valid[:, None, None]
    return jax.ops.segment_sum(prod, rows_index, num_segments=row_blocks)


def per_device(tiles, tile_rows, tile_cols, tile_counts, seed_pages, seed_mass, heat_time):
    n_row = lax.axis_size("row")
    n_col = lax.axis_size("col")
    slots = tiles.shape[2]
    tile_set = tiles.reshape(slots, 128, 128)
    rows_index = tile_rows.reshape(slots)
    cols_index = tile_cols.reshape(slots)
    valid = (jnp.arange(slots) < tile_counts.reshape(())).astype(jnp.float32)
    row_blocks = PB * n_col
    col_blocks = PB * n_row
    sets = seed_mass.shape[0]
    piece_pages = PB * 128
    my_row = lax.axis_index("row")
    my_col = lax.axis_index("col")
    first_page = (my_row * n_col + my_col) * piece_pages
    offset = seed_pages - first_page
    inside = (offset >= 0) & (offset < piece_pages)
    seed_ids = jnp.where(
        inside,
        jnp.arange(sets, dtype=jnp.int32)[:, None] * piece_pages + offset,
        sets * piece_pages,
    )
    placed = jax.ops.segment_sum(
        seed_mass.reshape(-1), seed_ids.reshape(-1), num_segments=sets * piece_pages + 1
    )
    value = placed[: sets * piece_pages].reshape(sets, PB, 128).transpose(1, 0, 2)
    column_sums = jnp.sum(tile_set, axis=1, dtype=jnp.float32) * valid[:, None]
    local_degree = jax.ops.segment_sum(column_sums, cols_index, num_segments=col_blocks)
    degree_group = 1.0 + lax.psum(local_degree, "row")
    scale = heat_time[None, :, None]
    total = value
    for step in range(K_TERMS):
        whole = lax.all_gather(value, "row", axis=0, tiled=True)
        column_z = (whole / degree_group[:, None, :]).astype(jnp.bfloat16)
        own_scaled = lax.dynamic_slice_in_dim(column_z, my_row * PB, PB, 0)
        partial_value = tile_image(column_z, tile_set, rows_index, cols_index, valid, row_blocks)
        image = lax.psum_scatter(partial_value, "col", scatter_dimension=0, tiled=True)
        value = scale / (step + 1.0) * (image + own_scaled.astype(jnp.float32))
        total = total + value
    return jnp.exp(-scale) * total


def solution(mesh):
    in_specs = (
        P(("parts", "row"), "col", None, None, None),
        P(("parts", "row"), "col", None),
        P(("parts", "row"), "col", None),
        P(("parts", "row"), "col"),
        P("parts", None),
        P("parts", None),
        P("parts"),
    )
    out_specs = P(("parts", "row", "col"), None, None)
    return jax.shard_map(
        per_device, mesh=mesh, in_specs=in_specs, out_specs=out_specs, check_vma=False
    )
```

profile of v0, /device:TPU:0, one launch (start us, length us, event | category | flops | bytes accessed | tf_op | source)
XLA Modules:
  0.0 147.9 jit_solution(11514916717099874507)
XLA Ops:
  6.5 0.8 compare_and_fusion
  10.4 2.8 %convert_reduce_fusion = f32[96,128]{1,0:T(8,128)S(1)} fusion(bf16[1,1,96,128,128]{4,3,2,1,0:T(8,128)(2,1)} %param.9), kind=kLoop, calls=%fused_computation.8 | loop fusion | flops 3133440 | bytes 3194880 | tf_op jit(solution)/shard_map/reduce_sum | solution.py:43
  13.2 1.3 scatter_custom_fusion.1
  14.5 12.9 %psum.7 = f32[64,128]{1,0:T(8,128)S(1)} all-reduce(f32[64,128]{1,0:T(8,128)S(1)} %scatter_custom_fusion.1), channel_id=1, replica_groups=mesh['parts'=2,'row'=4,'col'=4] {'row'}, use_global_device_ids=true, to_apply=%region_3.4 | all-reduce | flops 8192 | bytes 65536 | tf_op jit(solution)/shard_map/psum | solution.py:45
  27.4 2.2 %scatter_custom_fusion = f32[16385]{0:T(1024)S(1)} fusion(s32[256]{0:T(256)S(1)} %reshape.75, f32[256]{0:T(256)S(1)} %reshape.77, f32[]{:T(128)} %constant.20.clone.1), kind=kCustom, calls=%fused_computation.36 | custom fusion | flops 256 | bytes 65544 | tf_op jit(solution)/shard_map/scatter-add | solution.py:39
  30.2 5.8 %all_gather.9 = f32[64,8,128]{2,1,0:T(8,128)S(1)} all-gather(f32[16,8,128]{2,1,0:T(8,128)S(1)} %bitcast.29), channel_id=1, replica_groups=mesh['parts'=2,'row'=4,'col'=4] {'row'}, dimensions={0}, use_global_device_ids=true | all-gather | bytes 327680 | tf_op jit(solution)/shard_map/all_gather | solution.py:49
  36.8 2.5 %fusion.6 = f32[96,8,128]{2,1,0:T(8,128)} fusion(bf16[1,1,96,128,128]{4,3,2,1,0:T(8,128)(2,1)S(1)} %copy-done, bf16[96,8,128]{2,1,0:T(8,128)(2,1)S(1)} %gather_fusion, f32[96]{0:T(128)S(1)} %compare_convert_fusion, pred[96]{0:T(512)(128)(4,1)S(1)} %compare_and_fusion), kind=kOutput, calls=%fused_computation.15 | convolution fusion | flops 25362432 | bytes 3736032 | tf_op jit(solution)/shard_map/tsb,tab->tsa/dot_general | solution.py:12
  39.3 7.3 %scatter_fusion = f32[64,8,128]{2,1,0:T(8,128)S(1)} fusion(f32[64,8,128]{2,1,0:T(8,128)S(1)} %broadcast.39.clone.1, s32[96]{0:T(128)S(1)} %bitcast.30, f32[96,8,128]{2,1,0:T(8,128)} %fusion.6), kind=kCustom, calls=%fused_computation.5 | custom fusion | flops 98304 | bytes 1180032 | tf_op jit(solution)/shard_map/scatter-add | solution.py:14
  47.3 20.1 %reduce-scatter.4.cloned.1.call-done = f32[16,8,128]{2,1,0:T(8,128)} async-done(((f32[64,8,128]{2,1,0:T(8,128)}), f32[16,8,128]{2,1,0:T(8,128)}) %reduce-scatter.4.cloned.1.call-update) | async-done | bytes 65552 | tf_op jit(solution)/shard_map/reduce_scatter | solution.py:53
  67.4 0.9 add_multiply_fusion.2
  68.4 5.8 %all_gather.10 = f32[64,8,128]{2,1,0:T(8,128)S(1)} all-gather(f32[16,8,128]{2,1,0:T(8,128)S(1)} %add_multiply_fusion.2), channel_id=1, replica_groups=mesh['parts'=2,'row'=4,'col'=4] {'row'}, dimensions={0}, use_global_device_ids=true | all-gather | bytes 327680 | tf_op jit(solution)/shard_map/all_gather | solution.py:49
  74.1 0.8 divide_convert_fusion.1
  75.6 2.5 %fusion.9 = f32[96,8,128]{2,1,0:T(8,128)} fusion(bf16[1,1,96,128,128]{4,3,2,1,0:T(8,128)(2,1)S(1)} %copy-done, bf16[96,8,128]{2,1,0:T(8,128)(2,1)S(1)} %gather_fusion.1, f32[96]{0:T(128)S(1)} %compare_convert_fusion, pred[96]{0:T(512)(128)(4,1)S(1)} %compare_and_fusion), kind=kOutput, calls=%fused_computation.16 | convolution fusion | flops 25362432 | bytes 3736032 | tf_op jit(solution)/shard_map/tsb,tab->tsa/dot_general | solution.py:12
  78.2 7.3 %scatter_fusion.1 = f32[64,8,128]{2,1,0:T(8,128)S(1)} fusion(f32[64,8,128]{2,1,0:T(8,128)S(1)} %broadcast.39.clone, s32[96]{0:T(128)S(1)} %bitcast.31, f32[96,8,128]{2,1,0:T(8,128)} %fusion.9), kind=kCustom, calls=%fused_computation.6 | custom fusion | flops 98304 | bytes 1180032 | tf_op jit(solution)/shard_map/scatter-add | solution.py:14
  86.2 1.2 negate_exponential_fusion
  87.4 16.8 %reduce-scatter.6.cloned.1.call-done = f32[16,8,128]{2,1,0:T(8,128)} async-done(((f32[64,8,128]{2,1,0:T(8,128)}), f32[16,8,128]{2,1,0:T(8,128)}) %reduce-scatter.6.cloned.1.call-update) | async-done | bytes 65552 | tf_op jit(solution)/shard_map/reduce_scatter | solution.py:53
  104.2 0.9 add_multiply_fusion.1
  105.8 5.8 %all_gather.11 = f32[64,8,128]{2,1,0:T(8,128)S(1)} all-gather(f32[16,8,128]{2,1,0:T(8,128)S(1)} %add_multiply_fusion.1), channel_id=1, replica_groups=mesh['parts'=2,'row'=4,'col'=4] {'row'}, dimensions={0}, use_global_device_ids=true | all-gather | bytes 327680 | tf_op jit(solution)/shard_map/all_gather | solution.py:49
  111.5 0.8 divide_convert_fusion
  113.0 1.3 gather_fusion.2
  114.3 2.7 %fusion.12 = f32[96,8,128]{2,1,0:T(8,128)S(1)} fusion(bf16[1,1,96,128,128]{4,3,2,1,0:T(8,128)(2,1)S(1)} %copy-done, bf16[96,8,128]{2,1,0:T(8,128)(2,1)} %gather_fusion.2, f32[96]{0:T(128)S(1)} %compare_convert_fusion, pred[96]{0:T(512)(128)(4,1)S(1)} %compare_and_fusion), kind=kOutput, calls=%fused_computation.17 | convolution fusion | flops 25362432 | bytes 3736032 | tf_op jit(solution)/shard_map/tsb,tab->tsa/dot_general | solution.py:12
  117.0 3.8 %scatter_fusion.2 = f32[64,8,128]{2,1,0:T(8,128)S(1)} fusion(f32[64,8,128]{2,1,0:T(8,128)S(1)} %broadcast.39, s32[96]{0:T(128)S(1)} %bitcast.32, f32[96,8,128]{2,1,0:T(8,128)S(1)} %fusion.12), kind=kCustom, calls=%fused_computation.7 | custom fusion | flops 98304 | bytes 1180032 | tf_op jit(solution)/shard_map/scatter-add | solution.py:14
  121.6 18.1 %reduce-scatter.8.cloned.1.call-done = f32[16,8,128]{2,1,0:T(8,128)} async-done(((f32[64,8,128]{2,1,0:T(8,128)}), f32[16,8,128]{2,1,0:T(8,128)}) %reduce-scatter.8.cloned.1.call-update) | async-done | bytes 65552 | tf_op jit(solution)/shard_map/reduce_scatter | solution.py:53
  139.7 1.7 %add_multiply_fusion = f32[16,8,128]{2,1,0:T(8,128)} fusion(f32[16,8,128]{2,1,0:T(8,128)} %reduce-scatter.8.cloned.1.call-done, f32[16,8,128]{2,1,0:T(8,128)} %copy-done.6, f32[16,8,128]{2,1,0:T(8,128)} %copy-done.5, bf16[64,8,128]{2,1,0:T(8,128)(2,1)} %copy-done.4, s32[]{:T(128)S(6)} %select_n.17, f32[8]{0:T(128)} %get-tuple-element.7, ...), kind=kLoop, calls=%fused_computation.31 | loop fusion | flops 114688 | bytes 360516 | tf_op jit(solution)/shard_map/mul | solution.py:56
  (42 shorter events, 8.0 us)
Async XLA Ops:
  6.5 30.2 %copy-start = (bf16[1,1,96,128,128]{4,3,2,1,0:T(8,128)(2,1)S(1)}, bf16[1,1,96,128,128]{4,3,2,1,0:T(8,128)(2,1)}, u32[]{:S(2)}) copy-start(bf16[1,1,96,128,128]{4,3,2,1,0:T(8,128)(2,1)} %param.9) | copy-start | bytes 9437188
  6.5 60.9 %reduce-scatter.4.cloned.1.call-start = ((), (), s32[]{:S(2)}) async-start(), calls=%async_computation.3 | async-start | bytes 327680 | tf_op jit(solution)/shard_map/reduce_scatter | solution.py:53
  13.2 26.1 %copy-start.9 = (s32[1,1,96]{2,1,0:T(1,128)S(1)}, s32[1,1,96]{2,1,0:T(1,128)}, u32[]{:S(2)}) copy-start(s32[1,1,96]{2,1,0:T(1,128)} %param.10) | copy-start | bytes 1156
  27.4 8.7 %copy-start.8 = (f32[64,128]{1,0:T(8,128)}, f32[64,128]{1,0:T(8,128)S(1)}, u32[]{:S(2)}) copy-start(f32[64,128]{1,0:T(8,128)S(1)} %broadcast_add_fusion) | copy-start | bytes 98308
  29.6 0.6 copy-start.7
  46.6 0.7 copy-start.2
  47.3 56.9 %reduce-scatter.6.cloned.1.call-start = ((), (), s32[]{:S(2)}) async-start(), calls=%async_computation.4 | async-start | bytes 327680 | tf_op jit(solution)/shard_map/reduce_scatter | solution.py:53
  68.4 5.8 %copy-start.5 = (f32[16,8,128]{2,1,0:T(8,128)}, f32[16,8,128]{2,1,0:T(8,128)S(1)}, u32[]{:S(2)}) copy-start(f32[16,8,128]{2,1,0:T(8,128)S(1)} %add_multiply_fusion.2) | copy-start | bytes 196612
  85.4 0.7 copy-start.3
  86.1 53.6 %reduce-scatter.8.cloned.1.call-start = ((), (), s32[]{:S(2)}) async-start(), calls=%async_computation.5 | async-start | bytes 327680 | tf_op jit(solution)/shard_map/reduce_scatter | solution.py:53
  105.1 0.6 copy-start.6
  112.3 0.7 copy-start.4
  120.9 0.7 copy-start.1
Sparse Core Ops, SparseCore 0:
  47.4 19.9 reduce-scatter.3
  86.3 17.9 reduce-scatter.5
  121.7 17.9 reduce-scatter.7
where the time goes:
time: 149 us; the launch traced here: 148 us
  waiting for transfers between devices  55 us (37%)
  other arithmetic  33.4 us (22%)
  blocking collectives  30.2 us (20%)
  between operations  14 us (9%)
  matrix products  7.7 us (5%)
  local copies, waits for them, and re-layouts  7.54 us (5%)
    reduce_scatter x3, waiting for transfers between devices, per_device(): lax.psum_scatter(partial_value, 'col', scatter_dimension=0, tiled=True)  55 us
    scatter-add x3, other arithmetic, tile_image(): return jax.ops.segment_sum(prod, rows_index, num_segments=row_blocks)  18.4 us
    all_gather x3, blocking collectives, per_device(): whole = lax.all_gather(value, 'row', axis=0, tiled=True)  17.3 us
    psum x1, blocking collectives, per_device(): degree_group = 1.0 + lax.psum(local_degree, 'row')  12.9 us
    dot_general x3, matrix products, tile_image(): jnp.einsum('tsb,tab->tsa', picked, tile_set, preferred_element_type=jnp.f...  7.7 us
    unnamed x20, local copies, waits for them, and re-layouts  3.93 us
  transfers between devices with their start and end apart: 3, of which 3 were waited for; matrix products, arithmetic and copies ran while one was open for 1% of the time, Pallas kernels for 0%

commit v1 on v0

v1 whole, which is shorter than its diff:
```python
import functools

import jax
import jax.numpy as jnp
from jax import lax
from jax.experimental import pallas as pl
from jax.experimental.pallas import tpu as pltpu
from jax.sharding import PartitionSpec as P

PB = 16
K_TERMS = 3
LANES = 128
CHAINS = 2
MESH = pl.DeviceIdType.MESH


def kernel(
    n_row, n_col,
    tiles_hbm, rows_v, cols_v, cols_s, count_s, pages_v, mass_v, heat_s,
    out,
    tv, colsum, csend, crecv, degree, zf, zs, zr, chain0, chain1, ps, pr, idx_v, idx_s,
    tile_sem, idx_sem, c_send_sem, c_recv_sem, z_send_sem, z_recv_sem, p_send_sem, p_recv_sem,
):
    my_row = lax.axis_index("row")
    my_col = lax.axis_index("col")
    slots = tv.shape[0]
    sets = mass_v.shape[0]
    pieces = n_row * n_col
    chunks = tile_sem.shape[0]
    per_chunk = slots // chunks
    col_blocks = PB * n_row
    pairs = slots // 2

    def tile_copy(i):
        span = pl.ds(i * per_chunk, per_chunk)
        return pltpu.make_async_copy(tiles_hbm.at[0, 0, span], tv.at[span], tile_sem.at[i])

    for i in range(chunks):
        tile_copy(i).start()

    barrier = pltpu.get_barrier_semaphore()
    for d in range(1, n_row):
        pl.semaphore_signal(
            barrier, inc=1, device_id={"row": lax.rem(my_row + d, n_row)}, device_id_type=MESH
        )
    for d in range(1, n_col):
        pl.semaphore_signal(
            barrier, inc=1, device_id={"col": lax.rem(my_col + d, n_col)}, device_id_type=MESH
        )

    count = count_s[0, 0]
    rows_lane = rows_v[0]
    sub = lax.broadcasted_iota(jnp.int32, (slots, slots), 0)
    lane = lax.broadcasted_iota(jnp.int32, (slots, slots), 1)
    rows_sub = jnp.sum(
        jnp.where(sub == lane, jnp.broadcast_to(rows_lane, (slots, slots)), 0), axis=1, keepdims=True
    )
    same = (rows_sub == rows_lane) & (sub < lane) & ((sub & 1) == (lane & 1))
    idx_v[...] = jnp.zeros_like(idx_v)
    idx_v[0:1, 0:slots] = jnp.max(jnp.where(same, (sub >> 1) + 1, 0), axis=0, keepdims=True)
    wide = idx_v.shape[1]
    sub_w = lax.broadcasted_iota(jnp.int32, (slots, wide), 0)
    lane_w = lax.broadcasted_iota(jnp.int32, (slots, wide), 1)
    hit = (rows_sub == lane_w) & (sub_w < count)
    for p in range(CHAINS):
        found = jnp.where(hit & ((sub_w & 1) == p), (sub_w >> 1) + 1, 0)
        idx_v[1 + p : 2 + p, :] = jnp.max(found, axis=0, keepdims=True)
    idx_copy = pltpu.make_async_copy(idx_v, idx_s, idx_sem)
    idx_copy.start()

    def sum_chunk(i, carry):
        tile_copy(i).wait()
        for u in range(per_chunk // 8):
            span = pl.ds(pl.multiple_of(i * per_chunk + u * 8, 8), 8)
            colsum[span, :] = jnp.sum(tv[span].astype(jnp.float32), axis=1)
        return carry

    lax.fori_loop(0, chunks, sum_chunk, 0)
    block = lax.broadcasted_iota(jnp.int32, (col_blocks, slots), 0)
    slot = lax.broadcasted_iota(jnp.int32, (col_blocks, slots), 1)
    onehot = jnp.where((cols_v[0] == block) & (slot < count), 1.0, 0.0)
    csend[...] = jnp.dot(
        onehot, colsum[...], precision=lax.Precision.HIGHEST, preferred_element_type=jnp.float32
    )

    pl.semaphore_wait(barrier, n_row + n_col - 2)

    def c_copy(d):
        return pltpu.make_async_remote_copy(
            src_ref=csend, dst_ref=crecv.at[d - 1],
            send_sem=c_send_sem.at[d - 1], recv_sem=c_recv_sem.at[d - 1],
            device_id={"row": lax.rem(my_row + d, n_row)}, device_id_type=MESH,
        )

    for d in range(1, n_row):
        c_copy(d).start()

    set_id = lax.broadcasted_iota(jnp.int32, (sets, LANES), 0)
    page_lane = lax.broadcasted_iota(jnp.int32, (sets, LANES), 1)
    scale = jnp.zeros((sets, LANES), jnp.float32)
    for s in range(sets):
        scale = jnp.where(set_id == s, heat_s[s], scale)
    pages = pages_v[...]
    mass = mass_v[...]
    seeds = pages.shape[1]
    seed_lane = lax.broadcasted_iota(jnp.int32, pages.shape, 1)

    def seeds_of(piece):
        found = []
        for j in range(-(-seeds // pieces)):
            pick = seed_lane == piece + j * pieces
            offset = jnp.sum(jnp.where(pick, pages, 0), axis=1, keepdims=True) - piece * (PB * LANES)
            weight = jnp.sum(jnp.where(pick, mass, 0.0), axis=1, keepdims=True)
            found.append((offset - page_lane, jnp.broadcast_to(weight, (sets, LANES))))
        return found

    def seed_block(found, b):
        return sum(jnp.where(gap == b * LANES, weight, 0.0) for gap, weight in found)

    own = seeds_of(my_row * n_col + my_col)
    for b in range(PB):
        out[b] = seed_block(own, b)
    zero = jnp.zeros((sets, LANES), jnp.float32)
    chain0[0] = zero
    chain1[0] = zero

    idx_copy.wait()
    total = csend[...] + 1.0
    for d in range(1, n_row):
        c_copy(d).wait_recv()
        total = total + crecv[d - 1]
    degree[...] = total

    def seed_piece(r, carry):
        found = seeds_of(r * n_col + my_col)
        deg = degree[pl.ds(pl.multiple_of(r * PB, PB), PB), :]
        for b in range(PB):
            z = seed_block(found, b) / deg[b : b + 1, :]
            zf[r * PB + b] = z.astype(jnp.bfloat16).astype(jnp.float32)
        return carry

    lax.fori_loop(0, n_row, seed_piece, 0)

    def p_copy(k, d):
        return pltpu.make_async_remote_copy(
            src_ref=ps.at[k, d - 1], dst_ref=pr.at[k, d - 1],
            send_sem=p_send_sem.at[k, d - 1], recv_sem=p_recv_sem.at[k, d - 1],
            device_id={"col": lax.rem(my_col + d, n_col)}, device_id_type=MESH,
        )

    def z_copy(k, d):
        return pltpu.make_async_remote_copy(
            src_ref=zs.at[k], dst_ref=zr.at[k, d - 1],
            send_sem=z_send_sem.at[k, d - 1], recv_sem=z_recv_sem.at[k, d - 1],
            device_id={"row": lax.rem(my_row + d, n_row)}, device_id_type=MESH,
        )

    def row_sum(r):
        return chain0[idx_s[1, r]] + chain1[idx_s[2, r]]

    group = 12 if pairs % 12 == 0 else 1
    for k in range(K_TERMS):

        def multiply(g, carry):
            for u in range(group):
                j = g * group + u
                left = jnp.concatenate([zf[cols_s[0, 0, 2 * j]], zf[cols_s[0, 0, 2 * j + 1]]], axis=0)
                right = tv[pl.ds(2 * j, 2)].reshape(2 * LANES, LANES)
                prod = lax.dot_general(
                    left.astype(jnp.bfloat16), right, (((1,), (1,)), ((), ())),
                    preferred_element_type=jnp.float32,
                )
                chain0[j + 1] = prod[:sets, :LANES] + chain0[idx_s[0, 2 * j]]
                chain1[j + 1] = prod[sets:, LANES:] + chain1[idx_s[0, 2 * j + 1]]
            return carry

        lax.fori_loop(0, pairs // group, multiply, 0)

        def send_partial(d, carry):
            first = lax.rem(my_col + d, n_col) * PB
            for b in range(0, PB, 2):
                both = jnp.concatenate([row_sum(first + b), row_sum(first + b + 1)], axis=0)
                ps[k, d - 1, b * sets : (b + 2) * sets, :] = both.astype(jnp.bfloat16)
            p_copy(k, d).start()
            return carry

        lax.fori_loop(1, n_col, send_partial, 0)
        image = [row_sum(my_col * PB + b) + zf[my_row * PB + b] for b in range(PB)]
        for d in range(1, n_col):
            p_copy(k, d).wait_recv()
            for b in range(0, PB, 2):
                both = pr[k, d - 1, b * sets : (b + 2) * sets, :].astype(jnp.float32)
                image[b] = image[b] + both[:sets]
                image[b + 1] = image[b + 1] + both[sets:]
        factor = scale / (k + 1.0)
        value = [factor * x for x in image]
        if k == K_TERMS - 1:
            decay = jnp.exp(-scale)
            for b in range(PB):
                out[b] = decay * (out[b] + value[b])
            break
        deg = degree[pl.ds(pl.multiple_of(my_row * PB, PB), PB), :]
        for b in range(0, PB, 2):
            both = jnp.concatenate(
                [value[b] / deg[b : b + 1, :], value[b + 1] / deg[b + 1 : b + 2, :]], axis=0
            ).astype(jnp.bfloat16)
            zs[k, b * sets : (b + 2) * sets, :] = both
        for d in range(1, n_row):
            z_copy(k, d).start()

        def unpack(src, first):
            for b in range(0, PB, 2):
                both = src[b * sets : (b + 2) * sets, :].astype(jnp.float32)
                zf[first + b] = both[:sets]
                zf[first + b + 1] = both[sets:]

        unpack(zs.at[k], my_row * PB)
        for b in range(PB):
            out[b] = out[b] + value[b]
        for d in range(1, n_row):
            z_copy(k, d).wait_recv()
            unpack(zr.at[k, d - 1], lax.rem(my_row + n_row - d, n_row) * PB)

    for d in range(1, n_row):
        c_copy(d).wait_send()
        for k in range(K_TERMS - 1):
            z_copy(k, d).wait_send()
    for d in range(1, n_col):
        for k in range(K_TERMS):
            p_copy(k, d).wait_send()


def per_device(tiles, tile_rows, tile_cols, tile_counts, seed_pages, seed_mass, heat_time):
    n_row = lax.axis_size("row")
    n_col = lax.axis_size("col")
    slots = tiles.shape[2]
    sets = seed_mass.shape[0]
    chunks = 6 if slots % 48 == 0 else 1
    wide = max(LANES, PB * n_col)
    piece = (PB * sets, LANES)
    vmem = pl.BlockSpec(memory_space=pltpu.VMEM)
    smem = pl.BlockSpec(memory_space=pltpu.SMEM)
    dma = pltpu.SemaphoreType.DMA
    return pl.pallas_call(
        functools.partial(kernel, n_row, n_col),
        out_shape=jax.ShapeDtypeStruct((PB, sets, LANES), jnp.float32),
        in_specs=[pl.BlockSpec(memory_space=pl.ANY), vmem, vmem, smem, smem, vmem, vmem, smem],
        out_specs=vmem,
        scratch_shapes=[
            pltpu.VMEM((slots, LANES, LANES), jnp.bfloat16),
            pltpu.VMEM((slots, LANES), jnp.float32),
            pltpu.VMEM((PB * n_row, LANES), jnp.float32),
            pltpu.VMEM((n_row - 1, PB * n_row, LANES), jnp.float32),
            pltpu.VMEM((PB * n_row, LANES), jnp.float32),
            pltpu.VMEM((PB * n_row, sets, LANES), jnp.float32),
            pltpu.VMEM((K_TERMS - 1,) + piece, jnp.bfloat16),
            pltpu.VMEM((K_TERMS - 1, n_row - 1) + piece, jnp.bfloat16),
            pltpu.VMEM((slots // 2 + 1, sets, LANES), jnp.float32),
            pltpu.VMEM((slots // 2 + 1, sets, LANES), jnp.float32),
            pltpu.VMEM((K_TERMS, n_col - 1) + piece, jnp.bfloat16),
            pltpu.VMEM((K_TERMS, n_col - 1) + piece, jnp.bfloat16),
            pltpu.VMEM((8, wide), jnp.int32),
            pltpu.SMEM((8, wide), jnp.int32),
            dma((chunks,)),
            dma,
            dma((n_row - 1,)),
            dma((n_row - 1,)),
            dma((K_TERMS - 1, n_row - 1)),
            dma((K_TERMS - 1, n_row - 1)),
            dma((K_TERMS, n_col - 1)),
            dma((K_TERMS, n_col - 1)),
        ],
        compiler_params=pltpu.CompilerParams(
            collective_id=0, has_side_effects=True, vmem_limit_bytes=32 * 1024 * 1024
        ),
        name="heat_kernel",
    )(tiles, tile_rows, tile_cols, tile_cols, tile_counts, seed_pages, seed_mass, heat_time)


def solution(mesh):
    in_specs = (
        P(("parts", "row"), "col", None, None, None),
        P(("parts", "row"), "col", None),
        P(("parts", "row"), "col", None),
        P(("parts", "row"), "col"),
        P("parts", None),
        P("parts", None),
        P("parts"),
    )
    out_specs = P(("parts", "row", "col"), None, None)
    return jax.shard_map(
        per_device, mesh=mesh, in_specs=in_specs, out_specs=out_specs, check_vma=False
    )
```

time: 149 us -> 41 us (0.28)
  waiting for transfers between devices: 55 us -> 0 us
  Pallas kernels: 0 us -> 34.2 us
  other arithmetic: 33.4 us -> 0 us
  blocking collectives: 30.2 us -> 0 us
  between operations: 14 us -> 0.67 us
  matrix products: 7.7 us -> 0 us
  local copies, waits for them, and re-layouts: 7.54 us -> 5.85 us
    reduce_scatter x3 -> x0, waiting for transfers between devices: 55 us -> none  [per_device(): lax.psum_scatter(partial_value, 'col', scatter_dimension=0, tiled=True)]
    pallas_call x0 -> x1, Pallas kernels: none -> 34.2 us  [per_device(): pl.pallas_call(functools.partial(kernel, n_row, n_col), out_shape=jax.Sha...]
    scatter-add x5 -> x0, other arithmetic: 21.8 us -> none  [the longest x3 18.4 us: tile_image(): return jax.ops.segment_sum(prod, rows_index, num_segments=row_blocks)]
    all_gather x3 -> x0, blocking collectives: 17.3 us -> none  [per_device(): whole = lax.all_gather(value, 'row', axis=0, tiled=True)]
    psum x1 -> x0, blocking collectives: 12.9 us -> none  [per_device(): degree_group = 1.0 + lax.psum(local_degree, 'row')]
    dot_general x3 -> x0, matrix products: 7.7 us -> none  [tile_image(): jnp.einsum('tsb,tab->tsa', picked, tile_set, preferred_element_type=jnp.f...]
    mul x4 -> x0, other arithmetic: 3.5 us -> none  [the longest x2 1.83 us: per_device(): value = scale / (step + 1.0) * (image + own_scaled.astype(jnp.float32))]
    reduce_sum x1 -> x0, other arithmetic: 2.76 us -> none  [per_device(): column_sums = jnp.sum(tile_set, axis=1, dtype=jnp.float32) * valid[:, None]]
  transfers between devices with their start and end apart: 3 -> 0, of which waited for: 3 -> 0; matrix products, arithmetic and copies ran while one was open for 1% -> 0% of each run, Pallas kernels for 0% -> 0%
where the time goes in v1:
time: 41 us; the launch traced here: 40.8 us
  Pallas kernels  34.2 us (83%)
  local copies, waits for them, and re-layouts  5.85 us (14%)
  between operations  0.67 us (2%)
    pallas_call x1, Pallas kernels, per_device(): pl.pallas_call(functools.partial(kernel, n_row, n_col), out_shape=jax.Sha...  34.2 us
    unnamed x13, local copies, waits for them, and re-layouts  5.85 us

profile of v1, /device:TPU:0, one launch (start us, length us, event | category | flops | bytes accessed | tf_op | source)
XLA Modules:
  0.0 40.8 jit_solution(13595244048198031392)
XLA Ops:
  0.7 0.0 copy-start
  0.7 1.9 %copy-done = bf16[1,1,96,128,128]{4,3,2,1,0:T(8,128)(2,1)S(1)} copy-done((bf16[1,1,96,128,128]{4,3,2,1,0:T(8,128)(2,1)S(1)}, bf16[1,1,96,128,128]{4,3,2,1,0:T(8,128)(2,1)}, u32[]{:S(2)}) %copy-start) | copy-done | bytes 3145752
  2.5 0.0 copy-start.1
  2.5 0.7 %copy-done.1 = s32[8,32]{1,0:T(8,128)S(1)} copy-done((s32[8,32]{1,0:T(8,128)S(1)}, s32[8,32]{1,0:T(8,128)}, u32[]{:S(2)}) %copy-start.1) | copy-done | bytes 1048
  3.2 0.0 copy-start.2
  3.2 0.7 %copy-done.2 = f32[8,32]{1,0:T(8,128)S(1)} copy-done((f32[8,32]{1,0:T(8,128)S(1)}, f32[8,32]{1,0:T(8,128)}, u32[]{:S(2)}) %copy-start.2) | copy-done | bytes 1048
  3.9 0.0 copy-start.3
  3.9 0.7 %copy-done.3 = s32[1,1,96]{2,1,0:T(1,128)S(1)} copy-done((s32[1,1,96]{2,1,0:T(1,128)S(1)}, s32[1,1,96]{2,1,0:T(1,128)}, u32[]{:S(2)}) %copy-start.3) | copy-done | bytes 408
  4.6 0.0 copy-start.4
  4.6 0.7 %copy-done.4 = s32[1,1,96]{2,1,0:T(1,128)S(1)} copy-done((s32[1,1,96]{2,1,0:T(1,128)S(1)}, s32[1,1,96]{2,1,0:T(1,128)}, u32[]{:S(2)}) %copy-start.4) | copy-done | bytes 408
  5.2 0.0 copy-start.5
  5.2 0.7 %copy-done.5 = f32[8]{0:T(128)S(1)} copy-done((f32[8]{0:T(128)S(1)}, f32[8]{0:T(128)}, u32[]{:S(2)}) %copy-start.5) | copy-done | bytes 56
  5.9 34.2 %heat_kernel.1 = f32[16,8,128]{2,1,0:T(8,128)S(1)} custom-call(bf16[1,1,96,128,128]{4,3,2,1,0:T(8,128)(2,1)S(1)} %copy-done, s32[1,1,96]{2,1,0:T(1,128)S(1)} %copy-done.4, s32[1,1,96]{2,1,0:T(1,128)S(1)} %copy-done.3, s32[1,1,96]{2,1,0:T(1,128)S(1)} %copy-done.3, s32[1,1]{1,0:T(1,128)S(6)} %copy.9.count_s, s32[8,32]{1,0:T(8,128)S(1)} %copy-done.1, ...), custom_call_target="tpu_custom_call" | custom-call | tf_op jit(solution)/shard_map/heat_kernel/pallas_call | solution.py:244
  40.1 0.6 %copy.10 = f32[16,8,128]{2,1,0:T(8,128)} copy(f32[16,8,128]{2,1,0:T(8,128)S(1)} %heat_kernel.1) | data formatting | bytes 131072
Async XLA Ops:
  0.7 1.9 %copy-start = (bf16[1,1,96,128,128]{4,3,2,1,0:T(8,128)(2,1)S(1)}, bf16[1,1,96,128,128]{4,3,2,1,0:T(8,128)(2,1)}, u32[]{:S(2)}) copy-start(bf16[1,1,96,128,128]{4,3,2,1,0:T(8,128)(2,1)} %tiles_hbm.1) | copy-start | bytes 9437188
  2.5 0.7 %copy-start.1 = (s32[8,32]{1,0:T(8,128)S(1)}, s32[8,32]{1,0:T(8,128)}, u32[]{:S(2)}) copy-start(s32[8,32]{1,0:T(8,128)} %pages_v.1) | copy-start | bytes 3076
  3.2 0.7 %copy-start.2 = (f32[8,32]{1,0:T(8,128)S(1)}, f32[8,32]{1,0:T(8,128)}, u32[]{:S(2)}) copy-start(f32[8,32]{1,0:T(8,128)} %mass_v.1) | copy-start | bytes 3076
  3.9 0.7 %copy-start.3 = (s32[1,1,96]{2,1,0:T(1,128)S(1)}, s32[1,1,96]{2,1,0:T(1,128)}, u32[]{:S(2)}) copy-start(s32[1,1,96]{2,1,0:T(1,128)} %cols_s.1) | copy-start | bytes 1156
  4.6 0.7 %copy-start.4 = (s32[1,1,96]{2,1,0:T(1,128)S(1)}, s32[1,1,96]{2,1,0:T(1,128)}, u32[]{:S(2)}) copy-start(s32[1,1,96]{2,1,0:T(1,128)} %rows_v.1) | copy-start | bytes 1156
  5.2 0.7 %copy-start.5 = (f32[8]{0:T(128)S(1)}, f32[8]{0:T(128)}, u32[]{:S(2)}) copy-start(f32[8]{0:T(128)} %heat_s.1) | copy-start | bytes 100

commit v2 on v1

--- a/solution.py
+++ b/solution.py
@@ -16,9 +16,9 @@
 
 def kernel(
     n_row, n_col,
-    tiles_hbm, rows_v, cols_v, cols_s, count_s, pages_v, mass_v, heat_s,
+    tiles_hbm, rows_hbm, cols_hbm, count_hbm, pages_hbm, mass_hbm, heat_hbm,
     out,
-    tv, colsum, csend, crecv, degree, zf, zs, zr, chain0, chain1, ps, pr, idx_v, idx_s,
+    rows_v, cols_v, cols_s, count_s, pages_v, mass_v, heat_s, in_sem, tv, tt, colsum, csend, crecv, degree, zf, zs, zr, chain0, chain1, ps, pr, idx_v, idx_s,
     tile_sem, idx_sem, c_send_sem, c_recv_sem, z_send_sem, z_recv_sem, p_send_sem, p_recv_sem,
 ):
     my_row = lax.axis_index("row")
@@ -35,8 +35,19 @@
         span = pl.ds(i * per_chunk, per_chunk)
         return pltpu.make_async_copy(tiles_hbm.at[0, 0, span], tv.at[span], tile_sem.at[i])
 
+    loads = [
+        pltpu.make_async_copy(src, dst, in_sem.at[i])
+        for i, (src, dst) in enumerate([
+            (rows_hbm, rows_v), (count_hbm, count_s), (cols_hbm, cols_v), (cols_hbm, cols_s),
+            (pages_hbm, pages_v), (mass_hbm, mass_v), (heat_hbm, heat_s),
+        ])
+    ]
+    for load in loads:
+        load.start()
     for i in range(chunks):
         tile_copy(i).start()
+
+    near_last = sorted(range(1, n_row), key=lambda d: -min(d, n_row - d))
 
     barrier = pltpu.get_barrier_semaphore()
     for d in range(1, n_row):
@@ -48,7 +59,49 @@
             barrier, inc=1, device_id={"col": lax.rem(my_col + d, n_col)}, device_id_type=MESH
         )
 
+    for load in loads:
+        load.wait()
+
     count = count_s[0, 0]
+
+    def sum_chunk(i, carry):
+        tile_copy(i).wait()
+        for u in range(per_chunk // 8):
+            span = pl.ds(pl.multiple_of(i * per_chunk + u * 8, 8), 8)
+            colsum[span, :] = jnp.sum(tv[span].astype(jnp.float32), axis=1)
+        return carry
+
+    lax.fori_loop(0, chunks, sum_chunk, 0)
+    block = lax.broadcasted_iota(jnp.int32, (col_blocks, slots), 0)
+    slot = lax.broadcasted_iota(jnp.int32, (col_blocks, slots), 1)
+    onehot = jnp.where((cols_v[0] == block) & (slot < count), 1.0, 0.0)
+    csend[...] = jnp.dot(
+        onehot, colsum[...], precision=lax.Precision.HIGHEST, preferred_element_type=jnp.float32
+    )
+
+    pl.semaphore_wait(barrier, n_row + n_col - 2)
+
+    def c_copy(d):
+        return pltpu.make_async_remote_copy(
+            src_ref=csend, dst_ref=crecv.at[d - 1],
+            send_sem=c_send_sem.at[d - 1], recv_sem=c_recv_sem.at[d - 1],
+            device_id={"row": lax.rem(my_row + d, n_row)}, device_id_type=MESH,
+        )
+
+    for d in near_last:
+        c_copy(d).start()
+
+    turns = 8 if pairs % 8 == 0 else 1
+
+    def turn(g, carry):
+        for u in range(turns):
+            j = g * turns + u
+            tt[j, :, :LANES] = tv[2 * j].T
+            tt[j, :, LANES:] = tv[2 * j + 1].T
+        return carry
+
+    lax.fori_loop(0, pairs // turns, turn, 0)
+
     rows_lane = rows_v[0]
     sub = lax.broadcasted_iota(jnp.int32, (slots, slots), 0)
     lane = lax.broadcasted_iota(jnp.int32, (slots, slots), 1)
@@ -68,33 +121,6 @@
     idx_copy = pltpu.make_async_copy(idx_v, idx_s, idx_sem)
     idx_copy.start()
 
-    def sum_chunk(i, carry):
-        tile_copy(i).wait()
-        for u in range(per_chunk // 8):
-            span = pl.ds(pl.multiple_of(i * per_chunk + u * 8, 8), 8)
-            colsum[span, :] = jnp.sum(tv[span].astype(jnp.float32), axis=1)
-        return carry
-
-    lax.fori_loop(0, chunks, sum_chunk, 0)
-    block = lax.broadcasted_iota(jnp.int32, (col_blocks, slots), 0)
-    slot = lax.broadcasted_iota(jnp.int32, (col_blocks, slots), 1)
-    onehot = jnp.where((cols_v[0] == block) & (slot < count), 1.0, 0.0)
-    csend[...] = jnp.dot(
-        onehot, colsum[...], precision=lax.Precision.HIGHEST, preferred_element_type=jnp.float32
-    )
-
-    pl.semaphore_wait(barrier, n_row + n_col - 2)
-
-    def c_copy(d):
-        return pltpu.make_async_remote_copy(
-            src_ref=csend, dst_ref=crecv.at[d - 1],
-            send_sem=c_send_sem.at[d - 1], recv_sem=c_recv_sem.at[d - 1],
-            device_id={"row": lax.rem(my_row + d, n_row)}, device_id_type=MESH,
-        )
-
-    for d in range(1, n_row):
-        c_copy(d).start()
-
     set_id = lax.broadcasted_iota(jnp.int32, (sets, LANES), 0)
     page_lane = lax.broadcasted_iota(jnp.int32, (sets, LANES), 1)
     scale = jnp.zeros((sets, LANES), jnp.float32)
@@ -158,16 +184,15 @@
     def row_sum(r):
         return chain0[idx_s[1, r]] + chain1[idx_s[2, r]]
 
-    group = 12 if pairs % 12 == 0 else 1
+    group = 48 if pairs % 48 == 0 else 1
     for k in range(K_TERMS):
 
         def multiply(g, carry):
             for u in range(group):
                 j = g * group + u
                 left = jnp.concatenate([zf[cols_s[0, 0, 2 * j]], zf[cols_s[0, 0, 2 * j + 1]]], axis=0)
-                right = tv[pl.ds(2 * j, 2)].reshape(2 * LANES, LANES)
                 prod = lax.dot_general(
-                    left.astype(jnp.bfloat16), right, (((1,), (1,)), ((), ())),
+                    left.astype(jnp.bfloat16), tt[j], (((1,), (0,)), ((), ())),
                     preferred_element_type=jnp.float32,
                 )
                 chain0[j + 1] = prod[:sets, :LANES] + chain0[idx_s[0, 2 * j]]
@@ -205,7 +230,7 @@
                 [value[b] / deg[b : b + 1, :], value[b + 1] / deg[b + 1 : b + 2, :]], axis=0
             ).astype(jnp.bfloat16)
             zs[k, b * sets : (b + 2) * sets, :] = both
-        for d in range(1, n_row):
+        for d in near_last:
             z_copy(k, d).start()
 
         def unpack(src, first):
@@ -238,16 +263,23 @@
     chunks = 6 if slots % 48 == 0 else 1
     wide = max(LANES, PB * n_col)
     piece = (PB * sets, LANES)
-    vmem = pl.BlockSpec(memory_space=pltpu.VMEM)
-    smem = pl.BlockSpec(memory_space=pltpu.SMEM)
     dma = pltpu.SemaphoreType.DMA
     return pl.pallas_call(
         functools.partial(kernel, n_row, n_col),
         out_shape=jax.ShapeDtypeStruct((PB, sets, LANES), jnp.float32),
-        in_specs=[pl.BlockSpec(memory_space=pl.ANY), vmem, vmem, smem, smem, vmem, vmem, smem],
-        out_specs=vmem,
+        in_specs=[pl.BlockSpec(memory_space=pltpu.HBM)] * 7,
+        out_specs=pl.BlockSpec(memory_space=pltpu.VMEM),
         scratch_shapes=[
+            pltpu.VMEM(tile_rows.shape, jnp.int32),
+            pltpu.VMEM(tile_cols.shape, jnp.int32),
+            pltpu.SMEM(tile_cols.shape, jnp.int32),
+            pltpu.SMEM(tile_counts.shape, jnp.int32),
+            pltpu.VMEM(seed_pages.shape, jnp.int32),
+            pltpu.VMEM(seed_mass.shape, jnp.float32),
+            pltpu.SMEM(heat_time.shape, jnp.float32),
+            dma((7,)),
             pltpu.VMEM((slots, LANES, LANES), jnp.bfloat16),
+            pltpu.VMEM((slots // 2, LANES, 2 * LANES), jnp.bfloat16),
             pltpu.VMEM((slots, LANES), jnp.float32),
             pltpu.VMEM((PB * n_row, LANES), jnp.float32),
             pltpu.VMEM((n_row - 1, PB * n_row, LANES), jnp.float32),
@@ -271,10 +303,10 @@
             dma((K_TERMS, n_col - 1)),
         ],
         compiler_params=pltpu.CompilerParams(
-            collective_id=0, has_side_effects=True, vmem_limit_bytes=32 * 1024 * 1024
+            collective_id=0, has_side_effects=True, vmem_limit_bytes=60 * 1024 * 1024
         ),
         name="heat_kernel",
-    )(tiles, tile_rows, tile_cols, tile_cols, tile_counts, seed_pages, seed_mass, heat_time)
+    )(tiles, tile_rows, tile_cols, tile_counts, seed_pages, seed_mass, heat_time)
 
 
 def solution(mesh):

time: 41 us -> 34 us (0.83)
  local copies, waits for them, and re-layouts: 5.85 us -> 1.47 us
  Pallas kernels: 34.2 us -> 31.7 us
    unnamed x13 -> x1, local copies, waits for them, and re-layouts: 5.85 us -> 1.47 us
    pallas_call x1, Pallas kernels: 34.2 us -> 31.7 us  [per_device(): pl.pallas_call(functools.partial(kernel, n_row, n_col), out_shape=jax.Sha...]
where the time goes in v2:
time: 34 us; the launch traced here: 33.9 us
  Pallas kernels  31.7 us (93%)
  local copies, waits for them, and re-layouts  1.47 us (4%)
  between operations  0.66 us (2%)
    pallas_call x1, Pallas kernels, per_device(): pl.pallas_call(functools.partial(kernel, n_row, n_col), out_shape=jax.Sha...  31.7 us
    unnamed x1, local copies, waits for them, and re-layouts  1.47 us

profile of v2, /device:TPU:0, one launch (start us, length us, event | category | flops | bytes accessed | tf_op | source)
XLA Modules:
  0.0 33.9 jit_solution(14538042079029000391)
XLA Ops:
  0.7 31.7 %heat_kernel.1 = f32[16,8,128]{2,1,0:T(8,128)} custom-call(bf16[1,1,96,128,128]{4,3,2,1,0:T(8,128)(2,1)} %tiles_hbm.1, s32[1,1,96]{2,1,0:T(1,128)} %rows_hbm.1, s32[1,1,96]{2,1,0:T(1,128)} %cols_hbm.1, s32[1,1]{1,0:T(1,128)S(6)} %copy.9.count_hbm, s32[8,32]{1,0:T(8,128)} %pages_hbm.1, f32[8,32]{1,0:T(8,128)} %mass_hbm.1, f32[8]{0:T(128)} %heat_hbm.1), custom_call_target="tpu_custom_call" | custom-call | tf_op jit(solution)/shard_map/heat_kernel/pallas_call | solution.py:267
  32.4 1.5 %copy.10 = f32[16,8,128]{2,1,0:T(8,128)} copy(f32[16,8,128]{2,1,0:T(8,128)} %heat_kernel.1) | data formatting | bytes 131072

commit v3 on v2

--- a/solution.py
+++ b/solution.py
@@ -17,8 +17,8 @@
 def kernel(
     n_row, n_col,
     tiles_hbm, rows_hbm, cols_hbm, count_hbm, pages_hbm, mass_hbm, heat_hbm,
-    out,
-    rows_v, cols_v, cols_s, count_s, pages_v, mass_v, heat_s, in_sem, tv, tt, colsum, csend, crecv, degree, zf, zs, zr, chain0, chain1, ps, pr, idx_v, idx_s,
+    out_hbm,
+    out, out_sem, rows_v, cols_v, cols_s, count_s, pages_v, mass_v, heat_s, in_sem, tv, tt, colsum, csend, crecv, degree, zf, zs, zr, chain0, chain1, ps, pr, idx_v, idx_s,
     tile_sem, idx_sem, c_send_sem, c_recv_sem, z_send_sem, z_recv_sem, p_send_sem, p_recv_sem,
 ):
     my_row = lax.axis_index("row")
@@ -35,6 +35,20 @@
         span = pl.ds(i * per_chunk, per_chunk)
         return pltpu.make_async_copy(tiles_hbm.at[0, 0, span], tv.at[span], tile_sem.at[i])
 
+    near_last = sorted(range(1, n_row), key=lambda d: -min(d, n_row - d))
+
+    barrier = pltpu.get_barrier_semaphore()
+    for d in range(1, n_col):
+        pl.semaphore_signal(
+            barrier, inc=1, device_id={"col": lax.rem(my_col + d, n_col)}, device_id_type=MESH
+        )
+    for d in range(1, n_row):
+        pl.semaphore_signal(
+            barrier, inc=1, device_id={"row": lax.rem(my_row + d, n_row)}, device_id_type=MESH
+        )
+
+    for i in range(chunks):
+        tile_copy(i).start()
     loads = [
         pltpu.make_async_copy(src, dst, in_sem.at[i])
         for i, (src, dst) in enumerate([
@@ -44,20 +58,6 @@
     ]
     for load in loads:
         load.start()
-    for i in range(chunks):
-        tile_copy(i).start()
-
-    near_last = sorted(range(1, n_row), key=lambda d: -min(d, n_row - d))
-
-    barrier = pltpu.get_barrier_semaphore()
-    for d in range(1, n_row):
-        pl.semaphore_signal(
-            barrier, inc=1, device_id={"row": lax.rem(my_row + d, n_row)}, device_id_type=MESH
-        )
-    for d in range(1, n_col):
-        pl.semaphore_signal(
-            barrier, inc=1, device_id={"col": lax.rem(my_col + d, n_col)}, device_id_type=MESH
-        )
 
     for load in loads:
         load.wait()
@@ -90,17 +90,6 @@
 
     for d in near_last:
         c_copy(d).start()
-
-    turns = 8 if pairs % 8 == 0 else 1
-
-    def turn(g, carry):
-        for u in range(turns):
-            j = g * turns + u
-            tt[j, :, :LANES] = tv[2 * j].T
-            tt[j, :, LANES:] = tv[2 * j + 1].T
-        return carry
-
-    lax.fori_loop(0, pairs // turns, turn, 0)
 
     rows_lane = rows_v[0]
     sub = lax.broadcasted_iota(jnp.int32, (slots, slots), 0)
@@ -121,6 +110,17 @@
     idx_copy = pltpu.make_async_copy(idx_v, idx_s, idx_sem)
     idx_copy.start()
 
+    turns = 8 if pairs % 8 == 0 else 1
+
+    def turn(g, carry):
+        for u in range(turns):
+            j = g * turns + u
+            tt[j, :, :LANES] = tv[2 * j].T
+            tt[j, :, LANES:] = tv[2 * j + 1].T
+        return carry
+
+    lax.fori_loop(0, pairs // turns, turn, 0)
+
     set_id = lax.broadcasted_iota(jnp.int32, (sets, LANES), 0)
     page_lane = lax.broadcasted_iota(jnp.int32, (sets, LANES), 1)
     scale = jnp.zeros((sets, LANES), jnp.float32)
@@ -180,6 +180,12 @@
             send_sem=z_send_sem.at[k, d - 1], recv_sem=z_recv_sem.at[k, d - 1],
             device_id={"row": lax.rem(my_row + d, n_row)}, device_id_type=MESH,
         )
+
+    quarter = PB // 4
+
+    def out_copy(i):
+        span = pl.ds(i * quarter, quarter)
+        return pltpu.make_async_copy(out.at[span], out_hbm.at[span], out_sem.at[i])
 
     def row_sum(r):
         return chain0[idx_s[1, r]] + chain1[idx_s[2, r]]
@@ -223,6 +229,8 @@
             decay = jnp.exp(-scale)
             for b in range(PB):
                 out[b] = decay * (out[b] + value[b])
+                if b % quarter == quarter - 1:
+                    out_copy(b // quarter).start()
             break
         deg = degree[pl.ds(pl.multiple_of(my_row * PB, PB), PB), :]
         for b in range(0, PB, 2):
@@ -253,6 +261,8 @@
     for d in range(1, n_col):
         for k in range(K_TERMS):
             p_copy(k, d).wait_send()
+    for i in range(4):
+        out_copy(i).wait()
 
 
 def per_device(tiles, tile_rows, tile_cols, tile_counts, seed_pages, seed_mass, heat_time):
@@ -268,8 +278,10 @@
         functools.partial(kernel, n_row, n_col),
         out_shape=jax.ShapeDtypeStruct((PB, sets, LANES), jnp.float32),
         in_specs=[pl.BlockSpec(memory_space=pltpu.HBM)] * 7,
-        out_specs=pl.BlockSpec(memory_space=pltpu.VMEM),
+        out_specs=pl.BlockSpec(memory_space=pltpu.HBM),
         scratch_shapes=[
+            pltpu.VMEM((PB, sets, LANES), jnp.float32),
+            dma((4,)),
             pltpu.VMEM(tile_rows.shape, jnp.int32),
             pltpu.VMEM(tile_cols.shape, jnp.int32),
             pltpu.SMEM(tile_cols.shape, jnp.int32),

time: 34 us -> 34.2 us (level)
  no operation moved by 1% of the time
where the time goes in v3:
time: 34.2 us; the launch traced here: 34 us
  Pallas kernels  31.9 us (93%)
  local copies, waits for them, and re-layouts  1.47 us (4%)
  between operations  0.66 us (2%)
    pallas_call x1, Pallas kernels, per_device(): pl.pallas_call(functools.partial(kernel, n_row, n_col), out_shape=jax.Sha...  31.9 us
    unnamed x1, local copies, waits for them, and re-layouts  1.47 us

profile of v3, /device:TPU:0, one launch (start us, length us, event | category | flops | bytes accessed | tf_op | source)
XLA Modules:
  0.0 34.0 jit_solution(1585737651150636606)
XLA Ops:
  0.7 31.9 %heat_kernel.1 = f32[16,8,128]{2,1,0:T(8,128)} custom-call(bf16[1,1,96,128,128]{4,3,2,1,0:T(8,128)(2,1)} %tiles_hbm.1, s32[1,1,96]{2,1,0:T(1,128)} %rows_hbm.1, s32[1,1,96]{2,1,0:T(1,128)} %cols_hbm.1, s32[1,1]{1,0:T(1,128)S(6)} %copy.9.count_hbm, s32[8,32]{1,0:T(8,128)} %pages_hbm.1, f32[8,32]{1,0:T(8,128)} %mass_hbm.1, f32[8]{0:T(128)} %heat_hbm.1), custom_call_target="tpu_custom_call" | custom-call | tf_op jit(solution)/shard_map/heat_kernel/pallas_call | solution.py:277
  32.5 1.5 %copy.10 = f32[16,8,128]{2,1,0:T(8,128)} copy(f32[16,8,128]{2,1,0:T(8,128)} %heat_kernel.1) | data formatting | bytes 131072
